TPU v7x, 256 devices: a whole 4x4x8 slice. The times are simulated.
256 devices in a mesh: leaf: 16 (over z, core), row: 4 (over y), col: 4 (over x).
Axes of the slice: x: 4, y: 4, z: 8, core: 2. Of those that a mesh axis runs over, the one named last changes fastest.
Arguments:
- sketch_leaf: bfloat16 [131072, 256], P(('leaf', 'row'), 'col'), may hold values from -6 to 6
- sketch_sep: bfloat16 [8192, 256], P(('row', 'col')), may hold values from -6 to 6
- leaf_inverse: bfloat16 [131072, 8192], P(('leaf', 'col'), 'row'), as said below
- coupling: bfloat16 [131072, 2048], P(('leaf', 'col'), 'row'), may hold values from -0.0625 to 0.0625
- sep_inverse: bfloat16 [8192, 8192], P('leaf', ('row', 'col'))
- front_map: int32 [16, 16], replicated, may hold values from 0 to 63, as said below
Outputs:
- sketch_out_leaf: float32 [131072, 256], P(('leaf', 'row'), 'col')
- sketch_out_sep: float32 [8192, 256], P(('row', 'col'))
Inputs may be any that keep to these rules, and one draw needn't show every extreme that they name: `front_map`: row block q of every section's coupling lies in separator blocks q * 4 to q * 4 + 3. leaf_inverse and sep_inverse are inverses of lower triangular factor blocks (in natural order), stored in block-cyclic order.
All inputs are finite; a program needn't handle non-finite values.
Results may differ from a plain program's by a relative error of at most 0.024.
Values may be sent and summed in bfloat16 or wider, within the bound.
A program may use at most 64 MiB of HBM per device.

v0:
```python
import jax
import jax.numpy as jnp
from jax import lax
from jax.sharding import PartitionSpec as P


def contract_rows(left, right):
    return lax.dot_general(
        left, right, (((0,), (0,)), ((), ())), preferred_element_type=jnp.float32
    )


def shards(sketch_leaf, sketch_sep, leaf_inverse, coupling, sep_inverse, front_map):
    columns = sketch_leaf.shape[1] * lax.axis_size("col")
    q_index = lax.axis_index("row") * lax.axis_size("col") + lax.axis_index("col")
    section = lax.axis_index("leaf")
    partial_value = jnp.dot(
        leaf_inverse,
        lax.all_gather(sketch_leaf, "col", axis=1, tiled=True),
        preferred_element_type=jnp.float32,
    )
    front_z = lax.psum_scatter(partial_value, "row", scatter_dimension=1, tiled=True).astype(
        jnp.bfloat16
    )
    coupled_part = contract_rows(coupling, lax.all_gather(front_z, "row", axis=1, tiled=True))
    coupled = lax.psum_scatter(coupled_part, "col", scatter_dimension=0, tiled=True).astype(
        jnp.bfloat16
    )
    block_rows = coupled.shape[0]
    group = sketch_sep.shape[0] // block_rows
    own_slot = front_map[section, q_index] - q_index * group
    place = (jnp.arange(group, dtype=jnp.int32) == own_slot).astype(jnp.float32)
    spread = (place[:, None, None] * coupled.astype(jnp.float32)[None]).reshape(
        group * block_rows, columns
    )
    total = lax.psum(spread.astype(jnp.bfloat16), "leaf").astype(jnp.float32)
    sep_rhs = (sketch_sep.astype(jnp.float32) - total).astype(jnp.bfloat16)
    sep_part = jnp.dot(sep_inverse, sep_rhs, preferred_element_type=jnp.float32)
    sep_mid = lax.psum(sep_part.astype(jnp.bfloat16), ("row", "col"))
    sketch_out_sep = lax.psum(
        contract_rows(sep_inverse, sep_mid).astype(jnp.bfloat16), "leaf"
    ).astype(jnp.float32)
    sep_round = sketch_out_sep.astype(jnp.bfloat16)
    pulled = lax.dynamic_slice_in_dim(sep_round, own_slot * block_rows, block_rows, 0)
    back_part = jnp.dot(
        coupling,
        lax.all_gather(pulled, "col", axis=0, tiled=True),
        preferred_element_type=jnp.float32,
    )
    back_slice = lax.psum_scatter(
        back_part.astype(jnp.bfloat16), "row", scatter_dimension=1, tiled=True
    ).astype(jnp.float32)
    leaf_rhs = (front_z.astype(jnp.float32) - back_slice).astype(jnp.bfloat16)
    out_part = contract_rows(leaf_inverse, lax.all_gather(leaf_rhs, "row", axis=1, tiled=True))
    sketch_out_leaf = lax.psum_scatter(
        out_part.astype(jnp.bfloat16), "col", scatter_dimension=1, tiled=True
    ).astype(jnp.float32)
    return (sketch_out_leaf, sketch_out_sep)


def solution(mesh):
    placed = (
        P(("leaf", "row"), "col"),
        P(("row", "col"), None),
        P(("leaf", "col"), "row"),
        P(("leaf", "col"), "row"),
        P("leaf", ("row", "col")),
        P(),
    )
    return jax.shard_map(
        shards,
        mesh=mesh,
        in_specs=placed,
        out_specs=(P(("leaf", "row"), "col"), P(("row", "col"), None)),
        check_vma=False,
    )
```

profile of v0, /device:TPU:8, one launch (start us, length us, event | category | flops | bytes accessed | tf_op | source)
XLA Modules:
  0.0 567.1 jit_solution(8834700790642962263)
XLA Ops:
  8.0 31.3 %all-gather.4.cloned.1.call-done = bf16[2048,256]{0,1:T(8,128)(2,1)} async-done(((bf16[2048,64]{0,1:T(8,128)(2,1)}), bf16[2048,256]{0,1:T(8,128)(2,1)}) %all-gather.4.cloned.1.call-update) | async-done | bytes 1048592 | tf_op jit(solution)/shard_map/all_gather | solution.py:19
  39.2 7.3 %fusion.5 = f32[2048,256]{0,1:T(8,128)} fusion(bf16[2048,2048]{1,0:T(8,128)(2,1)} %param.8, bf16[2048,256]{0,1:T(8,128)(2,1)} %all-gather.4.cloned.1.call-done), kind=kOutput, calls=%fused_computation.17 | convolution fusion | flops 2147483648 | bytes 11534336 | tf_op jit(solution)/shard_map/dot_general | solution.py:17
  46.6 31.5 %reduce-scatter.5.cloned.1.call-done = f32[2048,64]{0,1:T(8,128)} async-done(((f32[2048,256]{0,1:T(8,128)}), f32[2048,64]{0,1:T(8,128)}) %reduce-scatter.5.cloned.1.call-update) | async-done | bytes 524304 | tf_op jit(solution)/shard_map/reduce_scatter | solution.py:22
  78.1 1.8 convert_element_type.68
  80.0 27.3 %all-gather.6.cloned.1.call-done = bf16[2048,256]{0,1:T(8,128)(2,1)} async-done(((bf16[2048,64]{0,1:T(8,128)(2,1)}), bf16[2048,256]{0,1:T(8,128)(2,1)}) %all-gather.6.cloned.1.call-update) | async-done | bytes 1048592 | tf_op jit(solution)/shard_map/all_gather | solution.py:25
  107.3 2.7 convolution_bitcast_fusion
  110.1 1.3 dynamic_slice.6
  112.1 23.5 %reduce-scatter.7.cloned.1.call-done = f32[128,256]{0,1:T(8,128)} async-done(((f32[512,256]{0,1:T(8,128)}), f32[128,256]{0,1:T(8,128)}) %reduce-scatter.7.cloned.1.call-update) | async-done | bytes 131088 | tf_op jit(solution)/shard_map/reduce_scatter | solution.py:26
  135.6 0.9 convert_convert_fusion
  137.5 109.2 %all-reduce.4.cloned.1.call-done = bf16[512,256]{1,0:T(8,128)(2,1)} async-done(((bf16[512,256]{1,0:T(8,128)(2,1)}), bf16[512,256]{1,0:T(8,128)(2,1)}) %all-reduce.4.cloned.1.call-update) | async-done | bytes 262160 | tf_op jit(solution)/shard_map/psum | solution.py:36
  246.7 2.0 fusion.2
  248.8 95.9 %all-reduce.6.cloned.1.call-done = bf16[512,256]{0,1:T(8,128)(2,1)} async-done(((bf16[512,256]{0,1:T(8,128)(2,1)}), bf16[512,256]{0,1:T(8,128)(2,1)}) %all-reduce.6.cloned.1.call-update) | async-done | bytes 262160 | tf_op jit(solution)/shard_map/psum | solution.py:39
  344.7 2.0 fusion.3
  346.7 109.1 %all-reduce.8.cloned.1.call-done = bf16[512,256]{0,1:T(8,128)(2,1)} async-done(((bf16[512,256]{0,1:T(8,128)(2,1)}), bf16[512,256]{0,1:T(8,128)(2,1)}) %all-reduce.8.cloned.1.call-update) | async-done | bytes 262160 | tf_op jit(solution)/shard_map/psum | solution.py:40
  455.8 0.8 constant_dynamic-slice_fusion
  456.7 12.0 %all_gather.14 = bf16[512,256]{0,1:T(8,128)(2,1)S(1)} all-gather(bf16[128,256]{0,1:T(8,128)(2,1)S(1)} %constant_dynamic-slice_fusion), channel_id=1, replica_groups=mesh['leaf'=16,'row'=4,'col'=4] {'col'}, dimensions={0}, use_global_device_ids=true | all-gather | bytes 327680 | tf_op jit(solution)/shard_map/all_gather | solution.py:47
  468.7 1.7 fusion.1
  470.5 23.6 %reduce-scatter.9.cloned.1.call-done = bf16[2048,64]{0,1:T(8,128)(2,1)} async-done(((bf16[2048,256]{0,1:T(8,128)(2,1)}), bf16[2048,64]{0,1:T(8,128)(2,1)}) %reduce-scatter.9.cloned.1.call-update) | async-done | bytes 262160 | tf_op jit(solution)/shard_map/reduce_scatter | solution.py:50
  494.0 1.7 subtract_convert_fusion
  495.8 28.2 %all-gather.8.cloned.1.call-done = bf16[2048,256]{0,1:T(8,128)(2,1)} async-done(((bf16[2048,64]{0,1:T(8,128)(2,1)}), bf16[2048,256]{0,1:T(8,128)(2,1)}) %all-gather.8.cloned.1.call-update) | async-done | bytes 1048592 | tf_op jit(solution)/shard_map/all_gather | solution.py:54
  524.0 7.0 %fusion = bf16[2048,256]{0,1:T(8,128)(2,1)} fusion(bf16[2048,256]{0,1:T(8,128)(2,1)} %all-gather.8.cloned.1.call-done, bf16[2048,2048]{1,0:T(8,128)(2,1)} %param.8), kind=kOutput, calls=%fused_computation.2 | convolution fusion | flops 2148007936 | bytes 10485760 | tf_op jit(solution)/shard_map/dot_general | solution.py:8
  531.0 0.9 copy.9
  532.0 26.5 %reduce-scatter.11.cloned.1.call-done = bf16[2048,64]{0,1:T(8,128)(2,1)} async-done(((bf16[2048,256]{0,1:T(8,128)(2,1)}), bf16[2048,64]{0,1:T(8,128)(2,1)}) %reduce-scatter.11.cloned.1.call-update) | async-done | bytes 262160 | tf_op jit(solution)/shard_map/reduce_scatter | solution.py:55
  558.5 1.8 convert_element_type.87
  (34 shorter events, 2.3 us)
Async XLA Ops:
  7.2 100.1 %copy-start = (bf16[2048,512]{1,0:T(8,128)(2,1)S(1)}, bf16[2048,512]{1,0:T(8,128)(2,1)}, u32[]{:S(2)}) copy-start(bf16[2048,512]{1,0:T(8,128)(2,1)} %param.9) | copy-start | bytes 6291460
  7.2 32.1 %all-gather.4.cloned.1.call-start = ((), (), s32[]{:S(2)}) async-start(), calls=%async_computation.4 | async-start | bytes 1310720 | tf_op jit(solution)/shard_map/all_gather | solution.py:19
  7.9 70.2 %reduce-scatter.5.cloned.1.call-start = ((), (), s32[]{:S(2)}) async-start(), calls=%async_computation.5 | async-start | bytes 2621440 | tf_op jit(solution)/shard_map/reduce_scatter | solution.py:22
  46.6 60.7 %all-gather.6.cloned.1.call-start = ((), (), s32[]{:S(2)}) async-start(), calls=%async_computation.6 | async-start | bytes 1310720 | tf_op jit(solution)/shard_map/all_gather | solution.py:25
  79.9 166.8 %copy-start.1 = (bf16[512,512]{1,0:T(8,128)(2,1)S(1)}, bf16[512,512]{1,0:T(8,128)(2,1)}, u32[]{:S(2)}) copy-start(bf16[512,512]{1,0:T(8,128)(2,1)} %param.10) | copy-start | bytes 1572868
  79.9 166.8 %copy-start.4 = (bf16[512,256]{1,0:T(8,128)(2,1)S(1)}, bf16[512,256]{1,0:T(8,128)(2,1)}, u32[]{:S(2)}) copy-start(bf16[512,256]{1,0:T(8,128)(2,1)} %param.7) | copy-start | bytes 786436
  79.9 55.7 %reduce-scatter.7.cloned.1.call-start = ((), (), s32[]{:S(2)}) async-start(), calls=%async_computation.7 | async-start | bytes 655360 | tf_op jit(solution)/shard_map/reduce_scatter | solution.py:26
  110.0 136.7 %all-reduce.4.cloned.1.call-start = ((), (), s32[]{:S(2)}) async-start(), calls=%async_computation.8 | async-start | bytes 524288 | tf_op jit(solution)/shard_map/psum | solution.py:36
  137.5 207.2 %all-reduce.6.cloned.1.call-start = ((), (), s32[]{:S(2)}) async-start(), calls=%async_computation.9 | async-start | bytes 524288 | tf_op jit(solution)/shard_map/psum | solution.py:39
  248.7 207.1 %all-reduce.8.cloned.1.call-start = ((), (), s32[]{:S(2)}) async-start(), calls=%async_computation.10 | async-start | bytes 524288 | tf_op jit(solution)/shard_map/psum | solution.py:40
  346.7 147.3 %reduce-scatter.9.cloned.1.call-start = ((), (), s32[]{:S(2)}) async-start(), calls=%async_computation.11 | async-start | bytes 1310720 | tf_op jit(solution)/shard_map/reduce_scatter | solution.py:50
  468.7 25.4 %copy-start.2 = (f32[2048,64]{0,1:T(8,128)S(1)}, f32[2048,64]{0,1:T(8,128)}, u32[]{:S(2)}) copy-start(f32[2048,64]{0,1:T(8,128)} %reduce-scatter.5.cloned.1.call-done) | copy-start | bytes 1572868
  470.4 53.6 %all-gather.8.cloned.1.call-start = ((), (), s32[]{:S(2)}) async-start(), calls=%async_computation.12 | async-start | bytes 1310720 | tf_op jit(solution)/shard_map/all_gather | solution.py:54
  495.7 35.3 %copy-start.3 = (bf16[512,256]{0,1:T(8,128)(2,1)S(1)}, bf16[512,256]{0,1:T(8,128)(2,1)}, u32[]{:S(2)}) copy-start(bf16[512,256]{0,1:T(8,128)(2,1)} %all-reduce.8.cloned.1.call-done) | copy-start | bytes 786436
  495.7 62.8 %reduce-scatter.11.cloned.1.call-start = ((), (), s32[]{:S(2)}) async-start(), calls=%async_computation.13 | async-start | bytes 1310720 | tf_op jit(solution)/shard_map/reduce_scatter | solution.py:55
Sparse Core Ops, SparseCore 0:
  9.8 29.3 all-gather.3
  46.7 31.3 reduce-scatter.4
  80.6 26.5 all-gather.5
  110.4 25.1 reduce-scatter.6
  138.4 108.2 all-reduce.3
  250.3 94.3 all-reduce.5
  347.7 108.0 all-reduce.7
  470.5 23.4 reduce-scatter.8
  496.5 27.3 all-gather.7
  531.1 27.3 reduce-scatter.10
where the time goes:
time: 568 us; the launch traced here: 567 us
  waiting for transfers between devices  507 us (89%)
  matrix products  22.8 us (4%)
  between operations  14.9 us (3%)
  blocking collectives  12 us (2%)
  other arithmetic  7 us (1%)
    psum x1, waiting for transfers between devices, shards(): total = lax.psum(spread.astype(jnp.bfloat16), 'leaf').astype(jnp.float32)  109 us
    psum x1, waiting for transfers between devices, shards(): lax.psum(contract_rows(sep_inverse, sep_mid).astype(jnp.bfloat16), 'leaf')  109 us
    psum x1, waiting for transfers between devices, shards(): sep_mid = lax.psum(sep_part.astype(jnp.bfloat16), ('row', 'col'))  95.9 us
    reduce_scatter x1, waiting for transfers between devices, shards(): lax.psum_scatter(partial_value, 'row', scatter_dimension=1, tiled=True)  31.5 us
    all_gather x1, waiting for transfers between devices, shards(): lax.all_gather(sketch_leaf, 'col', axis=1, tiled=True)  31.3 us
    all_gather x1, waiting for transfers between devices, shards(): lax.all_gather(leaf_rhs, 'row', axis=1, tiled=True)  28.2 us
    all_gather x1, waiting for transfers between devices, shards(): lax.all_gather(front_z, 'row', axis=1, tiled=True)  27.3 us
    reduce_scatter x1, waiting for transfers between devices, shards(): lax.psum_scatter(out_part.astype(jnp.bfloat16), 'col', scatter_dimension=...  26.5 us
  transfers between devices with their start and end apart: 10, of which 10 were waited for; matrix products, arithmetic and copies ran while one was open for 0% of the time, Pallas kernels for 0%

commit v1 on v0

v1 whole, which is shorter than its diff:
```python
import functools

import jax
import jax.numpy as jnp
from jax import lax
from jax.experimental import pallas as pl
from jax.experimental.pallas import tpu as pltpu
from jax.sharding import PartitionSpec as P

MESH = pl.DeviceIdType.MESH
BF16 = jnp.bfloat16
F32 = jnp.float32

N_LEAF, N_ROW, N_COL = 16, 4, 4
NZ = 8
LR = 2048
CM = 512
SQ = 512
BLK = 128
NC = 4
KT = 16
KC = 64
NG = 4
GC = NC // NG
GK = KC * GC
GT = GK // 4
TILE = 256

ORDER = (
    "L0", "L1", "L2", "Z0", "L3", "Z1", "Z2", "C0", "Z3", "U0", "C1", "C2", "U1", "V0",
    "C3", "U2", "S0", "U3", "V1", "S1", "V2", "M0", "S2", "V3", "M1", "S3", "T0", "M2",
    "T1", "M3", "O0", "T2", "O1", "T3", "P0", "O2", "P1", "B0", "O3", "B1", "P2", "R0",
    "P3", "B2", "R1", "Q0", "B3", "Y0", "R2", "Q1", "F0", "R3", "Q2", "F1", "Q3", "F2",
    "F3",
)


def nt(left, right):
    return lax.dot_general(left, right, (((1,), (1,)), ((), ())), preferred_element_type=F32)


def nn(left, right):
    return lax.dot_general(left, right, (((1,), (0,)), ((), ())), preferred_element_type=F32)


def kernel(
    xt, sep, lfac, cfac, sfac, fmap_in,
    out_leaf, out_sep,
    lv, cv, sv, sep_in, sept, ot, fmap, xg, zps, zr, zg, cps, cr, lr, prs, pr, mps, mr, mg, ops, orr, og, pg,
    bps, br, rg, fps, fr,
    load_sem, ssem, rsem,
):
    l, r, c = lax.axis_index("leaf"), lax.axis_index("row"), lax.axis_index("col")
    parity = lax.rem(l, 2)
    z = lax.div(l, 2)
    q = r * N_COL + c

    def xpeer(o):
        return (l, r, lax.rem(c + o, N_COL))

    def ypeer(o):
        return (l, lax.rem(r + o, N_ROW), c)

    def zpeer(o):
        return (lax.rem(l + 2 * o, N_LEAF), r, c)

    def leafpeer(o):
        return (lax.rem(l + o, N_LEAF), r, c)

    def planepeer(o):
        return (l, lax.rem(r + o // 4, N_ROW), lax.rem(c + o % 4, N_COL))

    partner = (l + 1 - 2 * parity, r, c)

    load_l = pltpu.make_async_copy(lfac, lv, load_sem.at[0])
    load_c = pltpu.make_async_copy(cfac, cv, load_sem.at[1])
    load_s = pltpu.make_async_copy(sfac, sv, load_sem.at[2])
    own_x = pltpu.make_async_copy(xt, xg.at[:, c], load_sem.at[3])
    load_sep = pltpu.make_async_copy(sep, sep_in, load_sem.at[4])
    load_map = pltpu.make_async_copy(fmap_in, fmap, load_sem.at[5])
    own_x.start()
    load_sep.start()
    load_map.start()
    load_l.start()
    load_c.start()
    load_s.start()

    barrier = pltpu.get_barrier_semaphore()
    for o in range(1, 16):
        pl.semaphore_signal(barrier, inc=1, device_id=leafpeer(o), device_id_type=MESH)
        pl.semaphore_signal(barrier, inc=1, device_id=planepeer(o), device_id_type=MESH)
    pl.semaphore_wait(barrier, 30)

    sent = []

    def send(src, dst, stage, at, device):
        pltpu.make_async_remote_copy(
            src_ref=src, dst_ref=dst, send_sem=ssem.at[stage, at], recv_sem=rsem.at[stage, at],
            device_id=device, device_id_type=MESH,
        ).start()

    def arrived(ref, stage, at):
        pltpu.make_async_copy(ref, ref, rsem.at[stage, at]).wait()
        sent.append((ref, stage, at))

    for k in range(NC):
        for o in (2, 1, 3):
            send(xt.at[k], xg.at[k, c], 0, k, xpeer(o))
    load_sep.wait()
    load_map.wait()
    sept[...] = sep_in[...].astype(F32).T.astype(BF16).reshape(4, NC, KT, SQ)
    own_x.wait()
    load_l.wait()

    def step_l(k):
        arrived(xg.at[k, pl.ds(0, 3)], 0, k)
        for i in range(LR // TILE):
            depth = (i + 1) * TILE
            part = nt(
                xg[k, :, :, :depth].reshape(KC, depth), lv[i * TILE : depth, :depth]
            )
            zps[k, :, :, i * TILE : depth] = part.astype(BF16).reshape(4, KT, TILE)
        for o in (2, 1, 3):
            peer = ypeer(o)
            send(zps.at[k, peer[1]], zr.at[k, o - 1], 1, k, peer)

    def step_z(k):
        arrived(zr.at[k], 1, k)
        total = zps[k, r].astype(F32)
        for o in range(3):
            total = total + zr[k, o].astype(F32)
        zg[k, r] = total.astype(BF16)
        for o in (2, 1, 3):
            send(zg.at[k, r], zg.at[k, r], 2, k, ypeer(o))

    def step_c(k):
        if k == 0:
            load_c.wait()
        arrived(zg.at[k, pl.ds(0, 3)], 2, k)
        part = nn(zg[k].reshape(KC, LR), cv[...]).astype(BF16)
        for b in range(4):
            cps[k, b] = part[:, b * BLK : (b + 1) * BLK]
        for o in (2, 1, 3):
            peer = xpeer(o)
            send(cps.at[k, peer[2]], cr.at[k, o - 1], 3, k, peer)

    def step_u(g):
        for kk in range(GC):
            k = g * GC + kk
            arrived(cr.at[k], 3, k)
            total = cps[k, c].astype(F32)
            for o in range(3):
                total = total + cr[k, o].astype(F32)
            lr[g, z, kk * KC : (kk + 1) * KC, :] = total.astype(BF16)
        for o in (4, 3, 5, 2, 6, 1, 7):
            send(lr.at[g, z], lr.at[g, z], 4, g, zpeer(o))

    def step_v(g):
        arrived(lr.at[g, pl.ds(0, NZ - 1)], 4, g)
        totals = [jnp.zeros((GK, BLK), F32) for _ in range(4)]
        for s in range(NZ):
            slot = fmap[2 * s + parity, q] - 4 * q
            block = lr[g, s].astype(F32)
            for b in range(4):
                totals[b] = totals[b] + block * jnp.where(slot == b, 1.0, 0.0)
        for b in range(4):
            prs[g, b] = totals[b].astype(BF16)
        send(prs.at[g], pr.at[g], 5, g, partner)

    def step_s(g):
        if g == 0:
            load_s.wait()
        arrived(pr.at[g], 5, g)
        rhs = []
        for b in range(4):
            block = sept[:, g, :, b * BLK : (b + 1) * BLK].reshape(GK, BLK).astype(F32)
            rhs.append((block - (prs[g, b].astype(F32) + pr[g, b].astype(F32))).astype(BF16))
        part = nt(jnp.concatenate(rhs, axis=1), sv[...]).astype(BF16)
        for a in range(4):
            for b in range(4):
                mps[g, a * 4 + b] = part[a * GT : (a + 1) * GT, b * BLK : (b + 1) * BLK]
        for o in (10, 6, 14, 9, 11, 2, 8, 5, 7, 13, 15, 1, 3, 4, 12):
            peer = planepeer(o)
            send(mps.at[g, peer[1] * 4 + peer[2]], mr.at[g, o - 1], 6, g, peer)

    def sum_of(own, others):
        total = own.astype(F32)
        for o in range(15):
            total = total + others(o).astype(F32)
        return total.astype(BF16)

    def wide(ref, g):
        return jnp.concatenate(
            [
                jnp.concatenate([ref[g, a * 4 + b] for a in range(4)], axis=0)
                for b in range(4)
            ],
            axis=1,
        )

    def step_m(g):
        arrived(mr.at[g], 6, g)
        mg[g, q] = sum_of(mps[g, q], lambda o: mr[g, o])
        for o in (10, 6, 14, 9, 11, 2, 8, 5, 7, 13, 15, 1, 3, 4, 12):
            send(mg.at[g, q], mg.at[g, q], 7, g, planepeer(o))

    def step_t(g):
        arrived(mg.at[g, pl.ds(0, 15)], 7, g)
        part = nn(wide(mg, g), sv[...]).astype(BF16)
        for a in range(4):
            for b in range(4):
                ops[g, a * 4 + b] = part[a * GT : (a + 1) * GT, b * BLK : (b + 1) * BLK]
        for o in (8, 7, 9, 6, 10, 5, 11, 4, 12, 3, 13, 2, 14, 1, 15):
            peer = leafpeer(o)
            send(ops.at[g, peer[0]], orr.at[g, o - 1], 8, g, peer)

    def step_o(g):
        arrived(orr.at[g], 8, g)
        og[g, l] = sum_of(ops[g, l], lambda o: orr[g, o])
        for o in (8, 7, 9, 6, 10, 5, 11, 4, 12, 3, 13, 2, 14, 1, 15):
            send(og.at[g, l], og.at[g, l], 9, g, leafpeer(o))

    def step_p(g):
        arrived(og.at[g, pl.ds(0, 15)], 9, g)
        full = wide(og, g).astype(F32)
        slot = fmap[l, q] - 4 * q
        pull = jnp.zeros((GK, BLK), F32)
        for b in range(4):
            pull = pull + full[:, b * BLK : (b + 1) * BLK] * jnp.where(slot == b, 1.0, 0.0)
        pg[g, c] = pull.astype(BF16)
        for o in (2, 1, 3):
            send(pg.at[g, c], pg.at[g, c], 10, g, xpeer(o))
        ot[:, g] = full.reshape(4, KT, SQ)

    def step_b(k):
        g, kk = k // GC, k % GC
        if kk == 0:
            arrived(pg.at[g, pl.ds(0, 3)], 10, g)
        rows = slice(kk * KC, (kk + 1) * KC)
        left = jnp.concatenate([pg[g, b, rows] for b in range(4)], axis=1)
        for i in range(LR // TILE):
            tile = slice(i * TILE, (i + 1) * TILE)
            bps[k, :, :, tile] = nt(left, cv[tile, :]).astype(BF16).reshape(4, KT, TILE)
        for o in (2, 1, 3):
            peer = ypeer(o)
            send(bps.at[k, peer[1]], br.at[k, o - 1], 11, k, peer)

    def step_r(k):
        arrived(br.at[k], 11, k)
        total = bps[k, r].astype(F32)
        for o in range(3):
            total = total + br[k, o].astype(F32)
        rg[k, r] = (zg[k, r].astype(F32) - total).astype(BF16)
        for o in (2, 1, 3):
            send(rg.at[k, r], rg.at[k, r], 12, k, ypeer(o))

    def step_q(k):
        arrived(rg.at[k, pl.ds(0, 3)], 12, k)
        for i in range(LR // TILE):
            first, last = i * TILE, (i + 1) * TILE
            part = nn(
                rg[k, :, :, first:].reshape(KC, LR - first), lv[first:, first:last]
            )
            fps[k, :, :, first:last] = part.astype(BF16).reshape(4, KT, TILE)
        for o in (2, 1, 3):
            peer = xpeer(o)
            send(fps.at[k, peer[2]], fr.at[k, o - 1], 13, k, peer)

    def step_f(k):
        arrived(fr.at[k], 13, k)
        total = fps[k, c].astype(F32)
        for o in range(3):
            total = total + fr[k, o].astype(F32)
        out_leaf[k] = total

    def step_y(_):
        out_sep[...] = ot[...].reshape(4 * NC * KT, SQ).T

    steps = dict(
        L=step_l, Z=step_z, C=step_c, U=step_u, V=step_v, S=step_s, M=step_m, T=step_t,
        O=step_o, P=step_p, B=step_b, R=step_r, Q=step_q, F=step_f, Y=step_y,
    )
    for name in ORDER:
        steps[name[0]](int(name[1]))

    for ref, stage, at in sent:
        pltpu.make_async_copy(ref, ref, ssem.at[stage, at]).wait()


def shards(sketch_leaf, sketch_sep, leaf_inverse, coupling, sep_inverse, front_map):
    xt = sketch_leaf.T.reshape(NC, KT, LR)
    vmem = pl.BlockSpec(memory_space=pltpu.VMEM)
    hbm = pl.BlockSpec(memory_space=pltpu.HBM)
    v = pltpu.VMEM
    leaf_wide = (NC, 4, KT, LR)
    leaf_got = (NC, 3, KT, LR)
    sep_full, sep_got = (NG, 16, GT, BLK), (NG, 15, GT, BLK)
    out_leaf, out_sep = pl.pallas_call(
        kernel,
        out_shape=(
            pltpu.VMEM((NC, KT, LR), F32),
            pltpu.VMEM((SQ, 4 * NC * KT), F32),
        ),
        in_specs=[hbm] * 6,
        out_specs=(vmem, vmem),
        scratch_shapes=[
            v((LR, LR), BF16), v((LR, CM), BF16), v((SQ, SQ), BF16),
            v((SQ, 4 * NC * KT), BF16), v((4, NC, KT, SQ), BF16), v((4, NC, KT, SQ), F32),
            pltpu.SMEM((N_LEAF, 16), jnp.int32),
            v(leaf_wide, BF16),
            v(leaf_wide, BF16), v(leaf_got, BF16), v(leaf_wide, BF16),
            v((NC, 4, KC, BLK), BF16), v((NC, 3, KC, BLK), BF16),
            v((NG, NZ, GK, BLK), BF16),
            v((NG, 4, GK, BLK), BF16), v((NG, 4, GK, BLK), BF16),
            v(sep_full, BF16), v(sep_got, BF16), v(sep_full, BF16),
            v(sep_full, BF16), v(sep_got, BF16), v(sep_full, BF16),
            v((NG, 4, GK, BLK), BF16),
            v(leaf_wide, BF16), v(leaf_got, BF16), v(leaf_wide, BF16),
            v(leaf_wide, BF16), v(leaf_got, BF16),
            pltpu.SemaphoreType.DMA((6,)),
            pltpu.SemaphoreType.DMA((14, NC)),
            pltpu.SemaphoreType.DMA((14, NC)),
        ],
        compiler_params=pltpu.CompilerParams(
            collective_id=0, has_side_effects=True, vmem_limit_bytes=58 << 20
        ),
        cost_estimate=pl.CostEstimate(
            flops=6_000_000_000, bytes_accessed=13_000_000, transcendentals=0
        ),
        name="sketch",
    )(xt, sketch_sep, leaf_inverse, coupling, sep_inverse, front_map)
    out_leaf = out_leaf.reshape(NC * KT, LR).T
    return out_leaf, out_sep


def solution(mesh):
    placed = (
        P(("leaf", "row"), "col"),
        P(("row", "col"), None),
        P(("leaf", "col"), "row"),
        P(("leaf", "col"), "row"),
        P("leaf", ("row", "col")),
        P(),
    )
    return jax.shard_map(
        shards,
        mesh=mesh,
        in_specs=placed,
        out_specs=(P(("leaf", "row"), "col"), P(("row", "col"), None)),
        check_vma=False,
    )
```

time: 568 us -> 102 us (0.18)
  waiting for transfers between devices: 507 us -> 0 us
  Pallas kernels: 0 us -> 99.3 us
  matrix products: 22.8 us -> 0 us
  between operations: 14.9 us -> 0.64 us
  blocking collectives: 12 us -> 0 us
  other arithmetic: 7 us -> 0 us
    psum x3 -> x0, waiting for transfers between devices: 314 us -> none  [the longest x1 109 us: shards(): total = lax.psum(spread.astype(jnp.bfloat16), 'leaf').astype(jnp.float32)]
    reduce_scatter x4 -> x0, waiting for transfers between devices: 105 us -> none  [the longest x1 31.5 us: shards(): lax.psum_scatter(partial_value, 'row', scatter_dimension=1, tiled=True)]
    pallas_call x0 -> x1, Pallas kernels: none -> 99.3 us  [shards(): pl.pallas_call(kernel, out_shape=(pltpu.VMEM((NC, KT, LR), F32), pltpu.VM...]
    all_gather x3 -> x0, waiting for transfers between devices: 86.7 us -> none  [the longest x1 31.3 us: shards(): lax.all_gather(sketch_leaf, 'col', axis=1, tiled=True)]
    dot_general x6 -> x0, matrix products: 22.8 us -> none  [the longest x3 11.7 us: contract_rows(): lax.dot_general(left, right, (((0,), (0,)), ((), ())), preferred_element_...]
    all_gather x1 -> x0, blocking collectives: 12 us -> none  [shards(): lax.all_gather(pulled, 'col', axis=0, tiled=True)]
    convert_element_type x6 -> x0, other arithmetic: 7 us -> none  [the longest x1 1.78 us: shards(): sketch_out_leaf = lax.psum_scatter(out_part.astype(jnp.bfloat16), 'col',...]
  transfers between devices with their start and end apart: 10 -> 0, of which waited for: 10 -> 0; matrix products, arithmetic and copies ran while one was open for 0% -> 0% of each run, Pallas kernels for 0% -> 0%
where the time goes in v1:
time: 102 us
  Pallas kernels  99.3 us (97%)
  local copies, waits for them, and re-layouts  1.59 us (2%)
    pallas_call x1, Pallas kernels, shards(): pl.pallas_call(kernel, out_shape=(pltpu.VMEM((NC, KT, LR), F32), pltpu.VM...  99.3 us

profile of v1, /device:TPU:8, one launch (start us, length us, event | category | flops | bytes accessed | tf_op | source)
XLA Modules:
  0.0 101.5 jit_solution(11005550675101244566)
XLA Ops:
  0.6 99.3 %sketch.1 = (f32[4,16,2048]{2,1,0:T(8,128)S(1)}, f32[512,256]{1,0:T(8,128)S(1)}) custom-call(bf16[4,16,2048]{2,1,0:T(8,128)(2,1)} %bitcast.7, bf16[512,256]{1,0:T(8,128)(2,1)} %sep.1, bf16[2048,2048]{1,0:T(8,128)(2,1)} %lfac.1, bf16[2048,512]{1,0:T(8,128)(2,1)} %cfac.1, bf16[512,512]{1,0:T(8,128)(2,1)} %sfac.1, s32[16,16]{1,0:T(8,128)} %fmap_in.1), custom_call_target="tpu_custom_call" | custom-call | flops 6000000000 | bytes 13000000 | tf_op jit(solution)/shard_map/sketch/pallas_call | solution.py:298
  99.9 0.8 copy.10
  100.7 0.8 copy.11

commit v2 on v1

--- a/solution.py
+++ b/solution.py
@@ -12,7 +12,6 @@
 F32 = jnp.float32
 
 N_LEAF, N_ROW, N_COL = 16, 4, 4
-NZ = 8
 LR = 2048
 CM = 512
 SQ = 512
@@ -23,15 +22,13 @@
 NG = 4
 GC = NC // NG
 GK = KC * GC
-GT = GK // 4
 TILE = 256
 
 ORDER = (
-    "L0", "L1", "L2", "Z0", "L3", "Z1", "Z2", "C0", "Z3", "U0", "C1", "C2", "U1", "V0",
-    "C3", "U2", "S0", "U3", "V1", "S1", "V2", "M0", "S2", "V3", "M1", "S3", "T0", "M2",
-    "T1", "M3", "O0", "T2", "O1", "T3", "P0", "O2", "P1", "B0", "O3", "B1", "P2", "R0",
-    "P3", "B2", "R1", "Q0", "B3", "Y0", "R2", "Q1", "F0", "R3", "Q2", "F1", "Q3", "F2",
-    "F3",
+    "L0", "L1", "L2", "Z0", "L3", "Z1", "Z2", "C0", "Z3", "U0", "C1", "C2", "U1", "S0",
+    "U2", "C3", "S1", "U3", "M0", "S2", "M1", "S3", "T0", "M2", "T1", "O0", "M3", "O1",
+    "T2", "P0", "T3", "O2", "P1", "B0", "O3", "B1", "P2", "R0", "P3", "B2", "Y0", "R1",
+    "B3", "Q0", "R2", "Q1", "F0", "R3", "Q2", "F1", "Q3", "F2", "F3",
 )
 
 
@@ -46,9 +43,9 @@
 def kernel(
     xt, sep, lfac, cfac, sfac, fmap_in,
     out_leaf, out_sep,
-    lv, cv, sv, sep_in, sept, ot, fmap, xg, zps, zr, zg, cps, cr, lr, prs, pr, mps, mr, mg, ops, orr, og, pg,
+    lv, cv, sw, sep_in, sept, ot, fmap, xg, zps, zr, zg, cps, cr, ccs, lr, mps, mr, mg, oq, og, pg,
     bps, br, rg, fps, fr,
-    load_sem, ssem, rsem,
+    load_sem, ssem, rsem, psend, precv,
 ):
     l, r, c = lax.axis_index("leaf"), lax.axis_index("row"), lax.axis_index("col")
     parity = lax.rem(l, 2)
@@ -61,20 +58,26 @@
     def ypeer(o):
         return (l, lax.rem(r + o, N_ROW), c)
 
-    def zpeer(o):
-        return (lax.rem(l + 2 * o, N_LEAF), r, c)
-
     def leafpeer(o):
         return (lax.rem(l + o, N_LEAF), r, c)
 
+    own_part = lax.rem(z, 2) * 2 + parity
+    side = 1 - 2 * lax.rem(z, 2)
+    tile_at = lax.div(z, 2)
+
+    def near(o):
+        return (lax.rem(l + 2 * o * side + N_LEAF, N_LEAF), r, c)
+
     def planepeer(o):
         return (l, lax.rem(r + o // 4, N_ROW), lax.rem(c + o % 4, N_COL))
 
     partner = (l + 1 - 2 * parity, r, c)
+    mate = near(1)
+    mate_partner = (mate[0] + 1 - 2 * parity, r, c)
 
     load_l = pltpu.make_async_copy(lfac, lv, load_sem.at[0])
     load_c = pltpu.make_async_copy(cfac, cv, load_sem.at[1])
-    load_s = pltpu.make_async_copy(sfac, sv, load_sem.at[2])
+    load_s = pltpu.make_async_copy(sfac, sw.at[0], load_sem.at[2])
     own_x = pltpu.make_async_copy(xt, xg.at[:, c], load_sem.at[3])
     load_sep = pltpu.make_async_copy(sep, sep_in, load_sem.at[4])
     load_map = pltpu.make_async_copy(fmap_in, fmap, load_sem.at[5])
@@ -86,10 +89,10 @@
     load_s.start()
 
     barrier = pltpu.get_barrier_semaphore()
-    for o in range(1, 16):
-        pl.semaphore_signal(barrier, inc=1, device_id=leafpeer(o), device_id_type=MESH)
-        pl.semaphore_signal(barrier, inc=1, device_id=planepeer(o), device_id_type=MESH)
-    pl.semaphore_wait(barrier, 30)
+    greeted = [planepeer(o) for o in range(1, 16)] + [leafpeer(o) for o in range(1, 16)]
+    for device in greeted:
+        pl.semaphore_signal(barrier, inc=1, device_id=device, device_id_type=MESH)
+    pl.semaphore_wait(barrier, len(greeted))
 
     sent = []
 
@@ -106,6 +109,24 @@
     for k in range(NC):
         for o in (2, 1, 3):
             send(xt.at[k], xg.at[k, c], 0, k, xpeer(o))
+    panels = []
+    for slot, device in ((3, near(-3)), (2, near(2)), (1, near(-1))):
+        for a in range(4):
+            area = (pl.ds(a * BLK, BLK), pl.ds(0, (a + 1) * BLK))
+            panels.append(
+                pltpu.make_async_remote_copy(
+                    src_ref=sfac.at[area], dst_ref=sw.at[(slot,) + area],
+                    send_sem=psend.at[len(panels)], recv_sem=precv.at[len(panels)],
+                    device_id=device, device_id_type=MESH,
+                )
+            )
+    waiting = list(panels)
+
+    def start_panels(count):
+        for _ in range(count):
+            waiting.pop(0).start()
+
+    start_panels(12)
     load_sep.wait()
     load_map.wait()
     sept[...] = sep_in[...].astype(F32).T.astype(BF16).reshape(4, NC, KT, SQ)
@@ -123,6 +144,7 @@
         for o in (2, 1, 3):
             peer = ypeer(o)
             send(zps.at[k, peer[1]], zr.at[k, o - 1], 1, k, peer)
+        start_panels(0)
 
     def step_z(k):
         arrived(zr.at[k], 1, k)
@@ -132,6 +154,8 @@
         zg[k, r] = total.astype(BF16)
         for o in (2, 1, 3):
             send(zg.at[k, r], zg.at[k, r], 2, k, ypeer(o))
+        if k == 0:
+            start_panels(0)
 
     def step_c(k):
         if k == 0:
@@ -145,86 +169,74 @@
             send(cps.at[k, peer[2]], cr.at[k, o - 1], 3, k, peer)
 
     def step_u(g):
-        for kk in range(GC):
-            k = g * GC + kk
-            arrived(cr.at[k], 3, k)
-            total = cps[k, c].astype(F32)
-            for o in range(3):
-                total = total + cr[k, o].astype(F32)
-            lr[g, z, kk * KC : (kk + 1) * KC, :] = total.astype(BF16)
-        for o in (4, 3, 5, 2, 6, 1, 7):
-            send(lr.at[g, z], lr.at[g, z], 4, g, zpeer(o))
-
-    def step_v(g):
-        arrived(lr.at[g, pl.ds(0, NZ - 1)], 4, g)
-        totals = [jnp.zeros((GK, BLK), F32) for _ in range(4)]
-        for s in range(NZ):
-            slot = fmap[2 * s + parity, q] - 4 * q
-            block = lr[g, s].astype(F32)
-            for b in range(4):
-                totals[b] = totals[b] + block * jnp.where(slot == b, 1.0, 0.0)
-        for b in range(4):
-            prs[g, b] = totals[b].astype(BF16)
-        send(prs.at[g], pr.at[g], 5, g, partner)
+        arrived(cr.at[g], 3, g)
+        total = cps[g, c].astype(F32)
+        for o in range(3):
+            total = total + cr[g, o].astype(F32)
+        ccs[g] = total.astype(BF16).reshape(4, KT, BLK)
+        lr[g, l] = ccs[g, tile_at]
+        for o in (8, 7, 9, 6, 10, 5, 11, 4, 12, 3, 13, 2, 14, 1, 15):
+            peer = leafpeer(o)
+            send(ccs.at[g, lax.div(peer[0], 4)], lr.at[g, l], 4, g, peer)
 
     def step_s(g):
         if g == 0:
             load_s.wait()
-        arrived(pr.at[g], 5, g)
-        rhs = []
-        for b in range(4):
-            block = sept[:, g, :, b * BLK : (b + 1) * BLK].reshape(GK, BLK).astype(F32)
-            rhs.append((block - (prs[g, b].astype(F32) + pr[g, b].astype(F32))).astype(BF16))
-        part = nt(jnp.concatenate(rhs, axis=1), sv[...]).astype(BF16)
-        for a in range(4):
+            for panel in panels:
+                panel.wait_recv()
+        arrived(lr.at[g, pl.ds(0, 15)], 4, g)
+        own = sept[tile_at, g].astype(F32)
+        rhs = [own[:, b * BLK : (b + 1) * BLK] for b in range(4)]
+        for s in range(N_LEAF):
+            slot = fmap[s, q] - 4 * q
+            block = lr[g, s].astype(F32)
             for b in range(4):
-                mps[g, a * 4 + b] = part[a * GT : (a + 1) * GT, b * BLK : (b + 1) * BLK]
+                rhs[b] = rhs[b] - block * jnp.where(slot == b, 1.0, 0.0)
+        rhs = jnp.concatenate(rhs, axis=1).astype(BF16)
+        for d in range(4):
+            for a in range(4):
+                depth = (a + 1) * BLK
+                part = nt(rhs[:, :depth], sw[d, a * BLK : depth, :depth])
+                mps[g, d * 4 + a] = part.astype(BF16)
         for o in (10, 6, 14, 9, 11, 2, 8, 5, 7, 13, 15, 1, 3, 4, 12):
             peer = planepeer(o)
             send(mps.at[g, peer[1] * 4 + peer[2]], mr.at[g, o - 1], 6, g, peer)
 
-    def sum_of(own, others):
-        total = own.astype(F32)
-        for o in range(15):
-            total = total + others(o).astype(F32)
-        return total.astype(BF16)
-
-    def wide(ref, g):
-        return jnp.concatenate(
-            [
-                jnp.concatenate([ref[g, a * 4 + b] for a in range(4)], axis=0)
-                for b in range(4)
-            ],
-            axis=1,
-        )
-
     def step_m(g):
         arrived(mr.at[g], 6, g)
-        mg[g, q] = sum_of(mps[g, q], lambda o: mr[g, o])
+        total = mps[g, q].astype(F32)
+        for o in range(15):
+            total = total + mr[g, o].astype(F32)
+        mg[g, q] = total.astype(BF16)
         for o in (10, 6, 14, 9, 11, 2, 8, 5, 7, 13, 15, 1, 3, 4, 12):
             send(mg.at[g, q], mg.at[g, q], 7, g, planepeer(o))
 
     def step_t(g):
         arrived(mg.at[g, pl.ds(0, 15)], 7, g)
-        part = nn(wide(mg, g), sv[...]).astype(BF16)
-        for a in range(4):
+        parts = [jnp.zeros((KT, BLK), F32) for _ in range(4)]
+        for d in range(4):
+            mid = jnp.concatenate([mg[g, d * 4 + b] for b in range(4)], axis=1)
             for b in range(4):
-                ops[g, a * 4 + b] = part[a * GT : (a + 1) * GT, b * BLK : (b + 1) * BLK]
-        for o in (8, 7, 9, 6, 10, 5, 11, 4, 12, 3, 13, 2, 14, 1, 15):
-            peer = leafpeer(o)
-            send(ops.at[g, peer[0]], orr.at[g, o - 1], 8, g, peer)
+                first, last = b * BLK, (b + 1) * BLK
+                parts[b] = parts[b] + nn(mid[:, first:], sw[d, first:, first:last])
+        oq[g, own_part] = jnp.concatenate(parts, axis=1).astype(BF16)
+        for device in (mate, mate_partner, partner):
+            send(oq.at[g, own_part], oq.at[g, own_part], 8, g, device)
 
     def step_o(g):
-        arrived(orr.at[g], 8, g)
-        og[g, l] = sum_of(ops[g, l], lambda o: orr[g, o])
-        for o in (8, 7, 9, 6, 10, 5, 11, 4, 12, 3, 13, 2, 14, 1, 15):
-            send(og.at[g, l], og.at[g, l], 9, g, leafpeer(o))
+        arrived(oq.at[g, pl.ds(0, 3)], 8, g)
+        total = oq[g, 0].astype(F32)
+        for o in range(1, 4):
+            total = total + oq[g, o].astype(F32)
+        og[g, tile_at] = total.astype(BF16)
+        for o in (3, 2, 1):
+            send(og.at[g, tile_at], og.at[g, tile_at], 9, g, near(-o))
 
     def step_p(g):
-        arrived(og.at[g, pl.ds(0, 15)], 9, g)
-        full = wide(og, g).astype(F32)
+        arrived(og.at[g, pl.ds(0, 3)], 9, g)
+        full = og[g].reshape(KC, SQ).astype(F32)
         slot = fmap[l, q] - 4 * q
-        pull = jnp.zeros((GK, BLK), F32)
+        pull = jnp.zeros((KC, BLK), F32)
         for b in range(4):
             pull = pull + full[:, b * BLK : (b + 1) * BLK] * jnp.where(slot == b, 1.0, 0.0)
         pg[g, c] = pull.astype(BF16)
@@ -277,7 +289,7 @@
         out_sep[...] = ot[...].reshape(4 * NC * KT, SQ).T
 
     steps = dict(
-        L=step_l, Z=step_z, C=step_c, U=step_u, V=step_v, S=step_s, M=step_m, T=step_t,
+        L=step_l, Z=step_z, C=step_c, U=step_u, S=step_s, M=step_m, T=step_t,
         O=step_o, P=step_p, B=step_b, R=step_r, Q=step_q, F=step_f, Y=step_y,
     )
     for name in ORDER:
@@ -285,6 +297,8 @@
 
     for ref, stage, at in sent:
         pltpu.make_async_copy(ref, ref, ssem.at[stage, at]).wait()
+    for panel in panels:
+        panel.wait_send()
 
 
 def shards(sketch_leaf, sketch_sep, leaf_inverse, coupling, sep_inverse, front_map):
@@ -294,7 +308,7 @@
     v = pltpu.VMEM
     leaf_wide = (NC, 4, KT, LR)
     leaf_got = (NC, 3, KT, LR)
-    sep_full, sep_got = (NG, 16, GT, BLK), (NG, 15, GT, BLK)
+    sep_full, sep_got = (NG, 16, KT, BLK), (NG, 15, KT, BLK)
     out_leaf, out_sep = pl.pallas_call(
         kernel,
         out_shape=(
@@ -304,22 +318,23 @@
         in_specs=[hbm] * 6,
         out_specs=(vmem, vmem),
         scratch_shapes=[
-            v((LR, LR), BF16), v((LR, CM), BF16), v((SQ, SQ), BF16),
+            v((LR, LR), BF16), v((LR, CM), BF16), v((4, SQ, SQ), BF16),
             v((SQ, 4 * NC * KT), BF16), v((4, NC, KT, SQ), BF16), v((4, NC, KT, SQ), F32),
             pltpu.SMEM((N_LEAF, 16), jnp.int32),
             v(leaf_wide, BF16),
             v(leaf_wide, BF16), v(leaf_got, BF16), v(leaf_wide, BF16),
             v((NC, 4, KC, BLK), BF16), v((NC, 3, KC, BLK), BF16),
-            v((NG, NZ, GK, BLK), BF16),
-            v((NG, 4, GK, BLK), BF16), v((NG, 4, GK, BLK), BF16),
+            v((NG, 4, KT, BLK), BF16), v((NG, N_LEAF, KT, BLK), BF16),
             v(sep_full, BF16), v(sep_got, BF16), v(sep_full, BF16),
-            v(sep_full, BF16), v(sep_got, BF16), v(sep_full, BF16),
+            v((NG, 4, KT, SQ), BF16), v((NG, 4, KT, SQ), BF16),
             v((NG, 4, GK, BLK), BF16),
             v(leaf_wide, BF16), v(leaf_got, BF16), v(leaf_wide, BF16),
             v(leaf_wide, BF16), v(leaf_got, BF16),
             pltpu.SemaphoreType.DMA((6,)),
             pltpu.SemaphoreType.DMA((14, NC)),
             pltpu.SemaphoreType.DMA((14, NC)),
+            pltpu.SemaphoreType.DMA((12,)),
+            pltpu.SemaphoreType.DMA((12,)),
         ],
         compiler_params=pltpu.CompilerParams(
             collective_id=0, has_side_effects=True, vmem_limit_bytes=58 << 20

time: 102 us -> 100 us (0.980)
  Pallas kernels: 99.3 us -> 97.7 us
    pallas_call x1, Pallas kernels: 99.3 us -> 97.7 us  [shards(): pl.pallas_call(kernel, out_shape=(pltpu.VMEM((NC, KT, LR), F32), pltpu.VM...]
where the time goes in v2:
time: 100 us
  Pallas kernels  97.7 us (98%)
  local copies, waits for them, and re-layouts  1.59 us (2%)
    pallas_call x1, Pallas kernels, shards(): pl.pallas_call(kernel, out_shape=(pltpu.VMEM((NC, KT, LR), F32), pltpu.VM...  97.7 us

profile of v2, /device:TPU:8, one launch (start us, length us, event | category | flops | bytes accessed | tf_op | source)
XLA Modules:
  0.0 100.0 jit_solution(9071336841475341425)
XLA Ops:
  0.6 97.7 %sketch.1 = (f32[4,16,2048]{2,1,0:T(8,128)S(1)}, f32[512,256]{1,0:T(8,128)S(1)}) custom-call(bf16[4,16,2048]{2,1,0:T(8,128)(2,1)} %bitcast.7, bf16[512,256]{1,0:T(8,128)(2,1)} %sep.1, bf16[2048,2048]{1,0:T(8,128)(2,1)} %lfac.1, bf16[2048,512]{1,0:T(8,128)(2,1)} %cfac.1, bf16[512,512]{1,0:T(8,128)(2,1)} %sfac.1, s32[16,16]{1,0:T(8,128)} %fmap_in.1), custom_call_target="tpu_custom_call" | custom-call | flops 6000000000 | bytes 13000000 | tf_op jit(solution)/shard_map/sketch/pallas_call | solution.py:312
  98.4 0.8 copy.10
  99.2 0.8 copy.11

commit v3 on v2

--- a/solution.py
+++ b/solution.py
@@ -26,9 +26,9 @@
 
 ORDER = (
     "L0", "L1", "L2", "Z0", "L3", "Z1", "Z2", "C0", "Z3", "U0", "C1", "C2", "U1", "S0",
-    "U2", "C3", "S1", "U3", "M0", "S2", "M1", "S3", "T0", "M2", "T1", "O0", "M3", "O1",
-    "T2", "P0", "T3", "O2", "P1", "B0", "O3", "B1", "P2", "R0", "P3", "B2", "Y0", "R1",
-    "B3", "Q0", "R2", "Q1", "F0", "R3", "Q2", "F1", "Q3", "F2", "F3",
+    "C3", "U2", "S1", "U3", "M0", "S2", "M1", "S3", "T0", "M2", "T1", "O0", "M3", "T2",
+    "O1", "P0", "O2", "T3", "P1", "B0", "O3", "P2", "B1", "B2", "R0", "P3", "R1", "Y0",
+    "B3", "R2", "Q0", "Q1", "R3", "F0", "Q2", "F1", "Q3", "F2", "F3",
 )
 
 
@@ -102,9 +102,14 @@
             device_id=device, device_id_type=MESH,
         ).start()
 
+    def left(ref, stage, at):
+        pltpu.make_async_copy(ref, ref, ssem.at[stage, at]).wait()
+
     def arrived(ref, stage, at):
         pltpu.make_async_copy(ref, ref, rsem.at[stage, at]).wait()
         sent.append((ref, stage, at))
+        if len(sent) > 8:
+            left(*sent.pop(0))
 
     for k in range(NC):
         for o in (2, 1, 3):
@@ -287,6 +292,8 @@
 
     def step_y(_):
         out_sep[...] = ot[...].reshape(4 * NC * KT, SQ).T
+        for panel in panels:
+            panel.wait_send()
 
     steps = dict(
         L=step_l, Z=step_z, C=step_c, U=step_u, S=step_s, M=step_m, T=step_t,
@@ -295,10 +302,8 @@
     for name in ORDER:
         steps[name[0]](int(name[1]))
 
-    for ref, stage, at in sent:
-        pltpu.make_async_copy(ref, ref, ssem.at[stage, at]).wait()
-    for panel in panels:
-        panel.wait_send()
+    for item in sent:
+        left(*item)
 
 
 def shards(sketch_leaf, sketch_sep, leaf_inverse, coupling, sep_inverse, front_map):

time: 100 us -> 100 us (level); the launches traced: 100 us -> 98.9 us
  Pallas kernels: 97.7 us -> 96.7 us
    pallas_call x1, Pallas kernels: 97.7 us -> 96.7 us  [shards(): pl.pallas_call(kernel, out_shape=(pltpu.VMEM((NC, KT, LR), F32), pltpu.VM...]
where the time goes in v3:
time: 100 us; the launch traced here: 98.9 us
  Pallas kernels  96.7 us (97%)
  local copies, waits for them, and re-layouts  1.59 us (2%)
    pallas_call x1, Pallas kernels, shards(): pl.pallas_call(kernel, out_shape=(pltpu.VMEM((NC, KT, LR), F32), pltpu.VM...  96.7 us

profile of v3, /device:TPU:8, one launch (start us, length us, event | category | flops | bytes accessed | tf_op | source)
XLA Modules:
  0.0 98.9 jit_solution(13618189102189631506)
XLA Ops:
  0.6 96.7 %sketch.1 = (f32[4,16,2048]{2,1,0:T(8,128)S(1)}, f32[512,256]{1,0:T(8,128)S(1)}) custom-call(bf16[4,16,2048]{2,1,0:T(8,128)(2,1)} %bitcast.7, bf16[512,256]{1,0:T(8,128)(2,1)} %sep.1, bf16[2048,2048]{1,0:T(8,128)(2,1)} %lfac.1, bf16[2048,512]{1,0:T(8,128)(2,1)} %cfac.1, bf16[512,512]{1,0:T(8,128)(2,1)} %sfac.1, s32[16,16]{1,0:T(8,128)} %fmap_in.1), custom_call_target="tpu_custom_call" | custom-call | flops 6000000000 | bytes 13000000 | tf_op jit(solution)/shard_map/sketch/pallas_call | solution.py:317
  97.3 0.8 copy.10
  98.1 0.8 copy.11
